TPU v7x, 128 devices: a whole 4x4x4 slice. The times are simulated.
128 devices in a mesh: row: 8 (over x, core), col: 16 (over y, z).
Axes of the slice: x: 4, y: 4, z: 4, core: 2. Of those that a mesh axis runs over, the one named last changes fastest.
Arguments:
- nodes: bfloat16 [8192, 512], P(('row', 'col')), may hold values from -6 to 6
- edges: bfloat16 [8, 16, 4096, 512], P('row', 'col'), may hold values from -6 to 6
- senders: int32 [8, 16, 4096], P('row', 'col'), may hold values from 0 to 511
- receivers: int32 [8, 16, 4096], P('row', 'col'), may hold values from 0 to 1023
- levels: int32 [8, 16, 4096], P('row', 'col'), may hold values from 0 to 6
- counts: int32 [8, 16], P('row', 'col'), may hold values from 1 to 4096, as said below
- edge_w1: bfloat16 [3, 512, 512], replicated, may hold values from -0.15625 to 0.15625
- level_bias: bfloat16 [7, 512], replicated, may hold values from -6 to 6
- edge_w2: bfloat16 [512, 512], replicated, may hold values from -0.25 to 0.25
- edge_gain: float32 [512], replicated, may hold values from 0.1 to 1.9
- node_w1: bfloat16 [2, 512, 512], replicated, may hold values from -0.1875 to 0.1875
- node_w2: bfloat16 [512, 512], replicated, may hold values from -0.25 to 0.25
- node_gain: float32 [512], replicated, may hold values from 0.1 to 1.9
- grid: bfloat16 [131072, 512], P(('row', 'col')), may hold values from -6 to 6
- send_rows: int32 [128, 128, 4], P(('row', 'col')), may hold values from 0 to 63, as said below
- dec_index: int32 [131072, 3], P(('row', 'col')), may hold values from 0 to 511, as said below
- dec_w1: bfloat16 [2, 512, 512], replicated, may hold values from -0.1875 to 0.1875
- dec_w2: bfloat16 [512, 512], replicated, may hold values from -0.25 to 0.25
- dec_gain: float32 [512], replicated, may hold values from 0.1 to 1.9
Outputs:
- nodes_out: bfloat16 [8192, 512], P(('row', 'col'))
- edges_out: bfloat16 [8, 16, 4096, 512], P('row', 'col')
- grid_out: bfloat16 [131072, 512], P(('row', 'col'))
Inputs may be any that keep to these rules, and one draw needn't show every extreme that they name: `senders`: at slots at or beyond the tile's count the index is arbitrary and unused. `receivers`: at slots at or beyond the tile's count the index is arbitrary and unused. `counts`: some tile is full in every draw. `send_rows`: the 4 rows that one device sends to one band device are distinct. `dec_index`: buffer rows are laid out by source device, then slot; every row of a band's buffer is named by some decoder edge of that band.
All inputs are finite; a program needn't handle non-finite values.
Results may differ from a plain program's by a relative error of at most 0.015.
Values may be sent and summed in bfloat16 or wider, within the bound.
No kernel may reach another device: no remote copies, remote signals or barrier semaphores. Data moves between devices by JAX's collectives and lax.ppermute only.
A program may use at most 128 MiB of HBM per device.

v0:
```python
import math
import jax
import jax.numpy as jnp
from jax import lax
from jax.sharding import PartitionSpec as P

EPSILON = 1e-05


def layer_norm(values, gain):
    center = values - jnp.mean(values, axis=-1, keepdims=True)
    spread = jnp.mean(center * center, axis=-1, keepdims=True)
    return center * lax.rsqrt(spread + EPSILON) * gain


def mlp_tail(pre, second_weight, gain):
    hidden = jax.nn.silu(pre).astype(jnp.bfloat16)
    output = jnp.dot(hidden, second_weight, preferred_element_type=jnp.float32)
    return layer_norm(output, gain)


def one_hot_rows(ids, count):
    return (ids[:, None] == jnp.arange(count, dtype=jnp.int32)[None, :]).astype(jnp.bfloat16)


def select_low(table_hot, table):
    return jnp.dot(table_hot, table, preferred_element_type=jnp.float32).astype(jnp.bfloat16)


def on_device(
    nodes,
    edges,
    senders,
    receivers,
    levels,
    counts,
    edge_w1,
    level_bias,
    edge_w2,
    edge_gain,
    node_w1,
    node_w2,
    node_gain,
    grid,
    send_rows,
    dec_index,
    dec_w1,
    dec_w2,
    dec_gain,
):
    node_block = nodes.shape[0]
    width = nodes.shape[1]
    capacity = edges.shape[2]
    level_count = level_bias.shape[0]
    sender_count = node_block * lax.axis_size("row")
    receiver_count = node_block * lax.axis_size("col")
    sender_block = lax.all_gather(nodes, "row", axis=0, tiled=True)
    receiver_block = lax.all_gather(nodes, "col", axis=0, tiled=True)
    joined_weight = edge_w1.reshape(3 * width, width)

    def first_layer(rows, send_hot, recv_hot):
        joined = jnp.concatenate(
            [rows, select_low(send_hot, sender_block), select_low(recv_hot, receiver_block)], axis=1
        )
        return jnp.dot(joined, joined_weight, preferred_element_type=jnp.float32)

    block_rows = math.gcd(capacity, 1024)
    block_count = capacity // block_rows
    slot_used = jnp.arange(capacity, dtype=jnp.int32) < counts[0, 0]
    items = (
        edges[0, 0].reshape(block_count, block_rows, width),
        senders[0, 0].reshape(block_count, block_rows),
        receivers[0, 0].reshape(block_count, block_rows),
        levels[0, 0].reshape(block_count, block_rows),
        slot_used.reshape(block_count, block_rows),
    )

    def edge_block(partial_value, item):
        rows, send_ids, recv_ids, level_ids, used = item
        send_hot = one_hot_rows(send_ids, sender_count)
        recv_hot = one_hot_rows(recv_ids, receiver_count)
        pre = first_layer(rows, send_hot, recv_hot)
        pre = pre + jnp.dot(
            one_hot_rows(level_ids, level_count), level_bias, preferred_element_type=jnp.float32
        )
        message = mlp_tail(pre, edge_w2, edge_gain).astype(jnp.bfloat16)
        kept = jnp.where(used[:, None], message, jnp.zeros((), jnp.bfloat16))
        updated = (rows.astype(jnp.float32) + kept.astype(jnp.float32)).astype(jnp.bfloat16)
        partial_value = partial_value + lax.dot_general(
            recv_hot, kept, (((0,), (0,)), ((), ())), preferred_element_type=jnp.float32
        )
        return (partial_value, updated)

    partial_value, edge_new = lax.scan(
        edge_block, jnp.zeros((receiver_count, width), jnp.float32), items
    )
    edges_out = edge_new.reshape(1, 1, capacity, width)
    summed = lax.psum(partial_value.astype(jnp.bfloat16), "col").astype(jnp.float32)
    aggregated = lax.dynamic_slice_in_dim(summed, lax.axis_index("col") * node_block, node_block, 0)
    node_pre = jnp.dot(nodes, node_w1[0], preferred_element_type=jnp.float32)
    node_pre = node_pre + jnp.dot(
        aggregated.astype(jnp.bfloat16), node_w1[1], preferred_element_type=jnp.float32
    )
    nodes_out = (nodes.astype(jnp.float32) + mlp_tail(node_pre, node_w2, node_gain)).astype(
        jnp.bfloat16
    )
    peers = send_rows.shape[1]
    per_peer = send_rows.shape[2]
    picked = select_low(one_hot_rows(send_rows[0].reshape(-1), node_block), nodes_out).reshape(
        peers, per_peer, width
    )
    received = lax.all_to_all(picked, ("row", "col"), split_axis=0, concat_axis=0, tiled=True)
    cells = grid.shape[0]
    fan_count = dec_index.shape[1]
    chosen = select_low(
        one_hot_rows(dec_index.reshape(-1), peers * per_peer),
        received.reshape(peers * per_peer, width),
    )
    node_dec = jnp.dot(chosen, dec_w1[1], preferred_element_type=jnp.float32).reshape(
        cells, fan_count, width
    )
    grid_part = jnp.dot(grid, dec_w1[0], preferred_element_type=jnp.float32)
    dec_pre = grid_part[:, None, :] + node_dec
    messages = mlp_tail(dec_pre.reshape(cells * fan_count, width), dec_w2, dec_gain).reshape(
        cells, fan_count, width
    )
    grid_out = (grid.astype(jnp.float32) + jnp.sum(messages, axis=1)).astype(jnp.bfloat16)
    return (nodes_out, edges_out, grid_out)


def solution(mesh):
    return jax.shard_map(
        on_device,
        mesh=mesh,
        in_specs=(
            P(("row", "col"), None),
            P("row", "col", None, None),
            P("row", "col", None),
            P("row", "col", None),
            P("row", "col", None),
            P("row", "col"),
            P(),
            P(),
            P(),
            P(),
            P(),
            P(),
            P(),
            P(("row", "col"), None),
            P(("row", "col"), None, None),
            P(("row", "col"), None),
            P(),
            P(),
            P(),
        ),
        out_specs=(P(("row", "col"), None), P("row", "col", None, None), P(("row", "col"), None)),
        check_vma=False,
    )
```

profile of v0, /device:TPU:1, one launch (start us, length us, event | category | flops | bytes accessed | tf_op | source)
XLA Modules:
  0.0 344.8 jit_solution(2025392052135723121)
XLA Ops:
  13.4 15.0 %all_gather.6 = bf16[512,512]{1,0:T(8,128)(2,1)S(1)} all-gather(bf16[64,512]{1,0:T(8,128)(2,1)} %param.21), channel_id=1, replica_groups=mesh['row'=8,'col'=16] {'row'}, dimensions={0}, use_global_device_ids=true | all-gather | bytes 589824 | tf_op jit(solution)/shard_map/all_gather | solution.py:57
  28.4 26.4 %all-gather.2.cloned.1.call-done = bf16[1024,512]{1,0:T(8,128)(2,1)} async-done(((bf16[64,512]{1,0:T(8,128)(2,1)}), bf16[1024,512]{1,0:T(8,128)(2,1)}) %all-gather.2.cloned.1.call-update) | async-done | bytes 1048592 | tf_op jit(solution)/shard_map/all_gather | solution.py:58
  54.8 99.2 %while.13 = (s32[]{:T(128)}, f32[1024,512]{1,0:T(8,128)}, bf16[4,1024,512]{2,1,0:T(8,128)(2,1)}, s32[4,1024]{1,0:T(4,128)S(1)}, pred[4,1024]{1,0:T(4,128)(4,1)S(...) while((s32[]{:T(128)}, f32[1024,512]{1,0:T(8,128)}, ...), condition=%wide.region_3.4_spmd.clone, body=%wide.region_0.3_spmd.clone.sunk | while | flops 4866973696 | bytes 48897348 | solution.py:94
  56.8 2.4 fusion.95
  62.1 5.2 %fusion.97 = f32[1024,512]{1,0:T(8,128)} fusion(bf16[1536,512]{1,0:T(8,128)(2,1)} %get-tuple-element.307, bf16[1024,512]{0,1:T(8,128)(2,1)} %fusion.95, bf16[1024,512]{0,1:T(8,128)(2,1)} %fusion.96, bf16[1024,512]{0,1:T(8,128)(2,1)S(1)} %bitcast.64), kind=kOutput, calls=%fused_computation.3.clone.1 | convolution fusion | flops 1620049920 | bytes 6815744 | tf_op jit(solution)/shard_map/while/body/eval_jaxpr/dot_general | solution.py:65
  67.3 2.9 fusion.98
  72.9 3.0 select_add_fusion.2
  80.4 2.4 fusion.95
  85.7 5.2 %fusion.97 = f32[1024,512]{1,0:T(8,128)} fusion(bf16[1536,512]{1,0:T(8,128)(2,1)} %get-tuple-element.307, bf16[1024,512]{0,1:T(8,128)(2,1)} %fusion.95, bf16[1024,512]{0,1:T(8,128)(2,1)} %fusion.96, bf16[1024,512]{0,1:T(8,128)(2,1)S(1)} %bitcast.64), kind=kOutput, calls=%fused_computation.3.clone.1 | convolution fusion | flops 1620049920 | bytes 6815744 | tf_op jit(solution)/shard_map/while/body/eval_jaxpr/dot_general | solution.py:65
  90.9 2.9 fusion.98
  96.5 4.6 %select_add_fusion.2 = f32[1024,512]{1,0:T(8,128)} fusion(f32[1024,512]{1,0:T(8,128)} %get-tuple-element.283, s32[1024]{0:T(1024)S(1)} %bitcast.67, pred[]{:T(512)S(6)} %compare.3, f32[1024,512]{0,1:T(8,128)S(1)} %get-tuple-element.264, f32[512]{0:T(512)S(1)} %copy-done.6, f32[1024]{0:T(1024)S(1)} %add_rsqrt_fusion.4, ...), kind=kOutput, calls=%fused_computation.10.clone.1 | convolution fusion | flops 1079508992 | bytes 6306817 | tf_op jit(solution)/shard_map/while/body/eval_jaxpr/dot_general | solution.py:89
  105.6 2.4 fusion.95
  110.9 5.2 %fusion.97 = f32[1024,512]{1,0:T(8,128)} fusion(bf16[1536,512]{1,0:T(8,128)(2,1)} %get-tuple-element.307, bf16[1024,512]{0,1:T(8,128)(2,1)} %fusion.95, bf16[1024,512]{0,1:T(8,128)(2,1)} %fusion.96, bf16[1024,512]{0,1:T(8,128)(2,1)S(1)} %bitcast.64), kind=kOutput, calls=%fused_computation.3.clone.1 | convolution fusion | flops 1620049920 | bytes 6815744 | tf_op jit(solution)/shard_map/while/body/eval_jaxpr/dot_general | solution.py:65
  116.1 2.9 fusion.98
  121.7 4.5 %select_add_fusion.2 = f32[1024,512]{1,0:T(8,128)} fusion(f32[1024,512]{1,0:T(8,128)} %get-tuple-element.283, s32[1024]{0:T(1024)S(1)} %bitcast.67, pred[]{:T(512)S(6)} %compare.3, f32[1024,512]{0,1:T(8,128)S(1)} %get-tuple-element.264, f32[512]{0:T(512)S(1)} %copy-done.6, f32[1024]{0:T(1024)S(1)} %add_rsqrt_fusion.4, ...), kind=kOutput, calls=%fused_computation.10.clone.1 | convolution fusion | flops 1079508992 | bytes 6306817 | tf_op jit(solution)/shard_map/while/body/eval_jaxpr/dot_general | solution.py:89
  136.1 5.2 %fusion.97 = f32[1024,512]{1,0:T(8,128)} fusion(bf16[1536,512]{1,0:T(8,128)(2,1)} %get-tuple-element.307, bf16[1024,512]{0,1:T(8,128)(2,1)} %fusion.95, bf16[1024,512]{0,1:T(8,128)(2,1)} %fusion.96, bf16[1024,512]{0,1:T(8,128)(2,1)S(1)} %bitcast.64), kind=kOutput, calls=%fused_computation.3.clone.1 | convolution fusion | flops 1620049920 | bytes 6815744 | tf_op jit(solution)/shard_map/while/body/eval_jaxpr/dot_general | solution.py:65
  141.3 2.9 fusion.98
  146.9 4.6 %select_add_fusion.2 = f32[1024,512]{1,0:T(8,128)} fusion(f32[1024,512]{1,0:T(8,128)} %get-tuple-element.283, s32[1024]{0:T(1024)S(1)} %bitcast.67, pred[]{:T(512)S(6)} %compare.3, f32[1024,512]{0,1:T(8,128)S(1)} %get-tuple-element.264, f32[512]{0:T(512)S(1)} %copy-done.6, f32[1024]{0:T(1024)S(1)} %add_rsqrt_fusion.4, ...), kind=kOutput, calls=%fused_computation.10.clone.1 | convolution fusion | flops 1079508992 | bytes 6306817 | tf_op jit(solution)/shard_map/while/body/eval_jaxpr/dot_general | solution.py:89
  154.1 2.8 convert_element_type.60
  157.4 86.1 %all-reduce.2.cloned.1.call-done = bf16[1024,512]{1,0:T(8,128)(2,1)} async-done(((bf16[1024,512]{1,0:T(8,128)(2,1)}), bf16[1024,512]{1,0:T(8,128)(2,1)}) %all-reduce.2.cloned.1.call-update) | async-done | bytes 1048592 | tf_op jit(solution)/shard_map/psum | solution.py:98
  246.4 8.8 %all-to-all-start = ((bf16[128,4,512]{2,1,0:T(4,128)(2,1)}), bf16[128,4,512]{2,1,0:T(4,128)(2,1)S(1)}, u32[]{:S(2)}, u32[]{:S(2)}) async-start(bf16[128,4,512]{2,1,0:T(4,128)(2,1)} %reshape.80), calls=%async_computation | async-start | bytes 1048576 | tf_op jit(solution)/shard_map/all_to_all | solution.py:112
  257.8 11.3 %all-to-all-done = bf16[128,4,512]{2,1,0:T(4,128)(2,1)S(1)} async-done(((bf16[128,4,512]{2,1,0:T(4,128)(2,1)}), bf16[128,4,512]{2,1,0:T(4,128)(2,1)S(1)}, u32[]{:S(2)}, u32[]{:S(2)}) %all-to-all-start) | async-done | bytes 524320 | tf_op jit(solution)/shard_map/all_to_all | solution.py:112
  270.0 4.7 %fusion.28 = bf16[3072,512]{1,0:T(8,128)(2,1)} fusion(bf16[512,512]{1,0:T(8,128)(2,1)} %reshape.81, s32[3072]{0:T(1024)S(1)} %eq.75), kind=kOutput, calls=%fused_computation.43 | convolution fusion | flops 1613758464 | bytes 3682304 | tf_op jit(solution)/shard_map/dot_general | solution.py:27
  274.7 9.1 %dot_general.50 = bf16[1024,3,512]{2,1,0:T(4,128)(2,1)} reshape(bf16[3072,512]{1,0:T(8,128)(2,1)} %fusion.28) | data formatting | bytes 6291456 | tf_op jit(solution)/shard_map/dot_general | solution.py:119
  283.8 4.4 %broadcast_add_fusion = f32[1024,3,512]{2,0,1:T(8,128)S(1)} fusion(f32[1024,512]{1,0:T(8,128)S(1)} %fusion.36, bf16[1024,3,512]{2,1,0:T(4,128)(2,1)} %dot_general.50, bf16[2,512,512]{2,1,0:T(8,128)(2,1)} %param.37), kind=kOutput, calls=%fused_computation.47 | convolution fusion | flops 1612185600 | bytes 13107200 | tf_op jit(solution)/shard_map/dot_general | solution.py:119
  288.2 7.5 %copy.29 = f32[1024,3,512]{2,1,0:T(4,128)} copy(f32[1024,3,512]{2,0,1:T(8,128)S(1)} %broadcast_add_fusion) | data formatting | bytes 12582912 | tf_op jit(solution)/shard_map/add | solution.py:123
  295.8 10.8 %reshape.82 = f32[3072,512]{1,0:T(8,128)} reshape(f32[1024,3,512]{2,1,0:T(4,128)} %copy.29) | data formatting | bytes 12582912 | tf_op jit(solution)/shard_map/reshape | solution.py:124
  306.5 4.1 %fusion.62 = (f32[3072]{0:T(1024)S(1)}, f32[3072,512]{1,0:T(8,128)S(1)}) fusion(bf16[512,512]{1,0:T(8,128)(2,1)S(1)} %copy-done, f32[3072,512]{1,0:T(8,128)} %reshape.82), kind=kOutput, calls=%fused_computation.81 | convolution fusion | flops 1620046848 | bytes 13119488 | tf_op jit(solution)/shard_map/dot_general | solution.py:18
  312.7 3.8 %multiply_multiply_fusion = f32[3072,512]{1,0:T(8,128)} fusion(f32[3072,512]{1,0:T(8,128)S(1)} %get-tuple-element.172, f32[512]{0:T(512)S(1)} %copy-done.9, f32[3072]{0:T(1024)S(1)} %add_rsqrt_fusion.1, f32[3072]{0:T(1024)S(1)} %broadcast_multiply_fusion.1), kind=kLoop, calls=%fused_computation.38 | loop fusion | flops 4718592 | bytes 12609536 | tf_op jit(solution)/shard_map/mul | solution.py:13
  316.5 10.5 %reshape.83 = f32[1024,3,512]{2,1,0:T(4,128)} reshape(f32[3072,512]{1,0:T(8,128)} %multiply_multiply_fusion) | data formatting | bytes 12582912 | tf_op jit(solution)/shard_map/reshape | solution.py:124
  327.0 8.4 %reduce_sum.67 = f32[1024,512]{1,0:T(8,128)S(1)} reduce(f32[1024,3,512]{2,1,0:T(4,128)} %reshape.83, f32[]{:T(128)} %constant.51.clone.1), dimensions={1}, to_apply=%region_9.10 | reduce | flops 1048576 | bytes 8388612 | tf_op jit(solution)/shard_map/reduce_sum | solution.py:127
  335.4 2.5 add_convert_fusion.1
  (138 shorter events, 57.0 us)
Async XLA Ops:
  7.2 299.4 %copy-start = (bf16[512,512]{1,0:T(8,128)(2,1)S(1)}, bf16[512,512]{1,0:T(8,128)(2,1)}, u32[]{:S(2)}) copy-start(bf16[512,512]{1,0:T(8,128)(2,1)} %param.38) | copy-start | bytes 1572868
  7.2 47.6 %all-gather.2.cloned.1.call-start = ((), (), s32[]{:S(2)}) async-start(), calls=%async_computation.1 | async-start | bytes 1114112 | tf_op jit(solution)/shard_map/all_gather | solution.py:58
  7.9 235.5 %all-reduce.2.cloned.1.call-start = ((), (), s32[]{:S(2)}) async-start(), calls=%async_computation.2 | async-start | bytes 2097152 | tf_op jit(solution)/shard_map/psum | solution.py:98
  54.8 2.0 copy-start.11
  61.1 1.0 copy-start.1
  62.1 5.2 %copy-start.13 = (bf16[7,512]{1,0:T(8,128)(2,1)S(1)}, bf16[7,512]{1,0:T(8,128)(2,1)}, u32[]{:S(2)}) copy-start(bf16[7,512]{1,0:T(8,128)(2,1)} %get-tuple-element.309) | copy-start | bytes 21508 | tf_op jit(solution)/shard_map/while
  70.2 1.2 copy-start.2
  70.2 1.2 copy-start.6
  78.4 2.0 copy-start.11
  84.7 1.0 copy-start.1
  85.7 5.2 %copy-start.13 = (bf16[7,512]{1,0:T(8,128)(2,1)S(1)}, bf16[7,512]{1,0:T(8,128)(2,1)}, u32[]{:S(2)}) copy-start(bf16[7,512]{1,0:T(8,128)(2,1)} %get-tuple-element.309) | copy-start | bytes 21508 | tf_op jit(solution)/shard_map/while
  93.8 1.2 copy-start.2
  93.8 1.2 copy-start.6
  103.6 2.0 copy-start.11
  109.9 1.0 copy-start.1
  110.9 5.2 %copy-start.13 = (bf16[7,512]{1,0:T(8,128)(2,1)S(1)}, bf16[7,512]{1,0:T(8,128)(2,1)}, u32[]{:S(2)}) copy-start(bf16[7,512]{1,0:T(8,128)(2,1)} %get-tuple-element.309) | copy-start | bytes 21508 | tf_op jit(solution)/shard_map/while
  119.0 1.2 copy-start.2
  119.0 1.2 copy-start.6
  128.8 2.0 copy-start.11
  135.1 1.0 copy-start.1
  136.1 5.2 %copy-start.13 = (bf16[7,512]{1,0:T(8,128)(2,1)S(1)}, bf16[7,512]{1,0:T(8,128)(2,1)}, u32[]{:S(2)}) copy-start(bf16[7,512]{1,0:T(8,128)(2,1)} %get-tuple-element.309) | copy-start | bytes 21508 | tf_op jit(solution)/shard_map/while
  144.2 1.2 copy-start.2
  144.2 1.2 copy-start.6
  154.0 2.9 copy-start.10
  154.0 3.1 copy-start.3
  154.0 3.1 copy-start.4
  154.0 89.4 %copy-start.12 = (bf16[512,512]{1,0:T(8,128)(2,1)S(1)}, bf16[512,512]{1,0:T(8,128)(2,1)}, u32[]{:S(2)}) copy-start(bf16[512,512]{1,0:T(8,128)(2,1)} %param.32) | copy-start | bytes 1572868
  156.9 88.1 %copy-start.8 = (f32[512]{0:T(512)S(1)}, f32[512]{0:T(512)}, u32[]{:S(2)}) copy-start(f32[512]{0:T(512)} %param.33) | copy-start | bytes 6148
  157.4 97.9 %copy-start.7 = (s32[1024,3]{0,1:T(4,128)S(1)}, s32[1024,3]{0,1:T(4,128)}, u32[]{:S(2)}) copy-start(s32[1024,3]{0,1:T(4,128)} %param.36) | copy-start | bytes 36868
  245.1 12.7 %copy-start.5 = (bf16[64,512]{1,0:T(8,128)(2,1)}, bf16[64,512]{1,0:T(8,128)(2,1)S(1)}, u32[]{:S(2)}) copy-start(bf16[64,512]{1,0:T(8,128)(2,1)S(1)} %add_convert_fusion.2) | copy-start | bytes 196612
  246.4 22.7 %all-to-all-start = ((bf16[128,4,512]{2,1,0:T(4,128)(2,1)}), bf16[128,4,512]{2,1,0:T(4,128)(2,1)S(1)}, u32[]{:S(2)}, u32[]{:S(2)}) async-start(bf16[128,4,512]{2,1,0:T(4,128)(2,1)} %reshape.80), calls=%async_computation | async-start | bytes 1048576 | tf_op jit(solution)/shard_map/all_to_all | solution.py:112
  310.7 2.0 copy-start.9
Sparse Core Ops, SparseCore 0:
  10.2 44.6 all-gather.1
  157.0 86.3 all-reduce.1
where the time goes:
time: 347 us; the launch traced here: 345 us
  waiting for transfers between devices  124 us (36%)
  matrix products  83.5 us (24%)
  local copies, waits for them, and re-layouts  66.4 us (19%)
  other arithmetic  31.3 us (9%)
  blocking collectives  15 us (4%)
  between operations  14.9 us (4%)
  starting transfers between devices  8.92 us (3%)
    psum x1, waiting for transfers between devices, on_device(): lax.psum(partial_value.astype(jnp.bfloat16), 'col').astype(jnp.float32)  86.1 us
    all_gather x1, waiting for transfers between devices, on_device(): receiver_block = lax.all_gather(nodes, 'col', axis=0, tiled=True)  26.4 us
    dot_general x10, matrix products, select_low(): jnp.dot(table_hot, table, preferred_element_type=jnp.float32)  22.4 us
    dot_general x4, matrix products, first_layer(): return jnp.dot(joined, joined_weight, preferred_element_type=jnp.float32)  20.7 us
    dot_general x6, matrix products, mlp_tail(): output = jnp.dot(hidden, second_weight, preferred_element_type=jnp.float32)  17.1 us
    dot_general x4, matrix products, edge_block(): lax.dot_general(recv_hot, kept, (((0,), (0,)), ((), ())), preferred_eleme...  16.6 us
    all_gather x1, blocking collectives, on_device(): sender_block = lax.all_gather(nodes, 'row', axis=0, tiled=True)  15 us
    all_to_all x1, waiting for transfers between devices, on_device(): lax.all_to_all(picked, ('row', 'col'), split_axis=0, concat_axis=0, tiled...  11.3 us
  transfers between devices with their start and end apart: 3, of which 3 were waited for; matrix products, arithmetic and copies ran while one was open for 2% of the time, Pallas kernels for 0%

commit v1 on v0

--- a/solution.py
+++ b/solution.py
@@ -5,6 +5,9 @@
 from jax.sharding import PartitionSpec as P
 
 EPSILON = 1e-05
+refer_rounds = lambda dimension_no, m: jnp.concatenate(
+    lax.all_to_all(jnp.stack(lax.axis_size("col") * [m], axis=0), "col", 0, 0), axis=dimension_no
+)
 
 
 def layer_norm(values, gain):
@@ -55,7 +58,7 @@
     sender_count = node_block * lax.axis_size("row")
     receiver_count = node_block * lax.axis_size("col")
     sender_block = lax.all_gather(nodes, "row", axis=0, tiled=True)
-    receiver_block = lax.all_gather(nodes, "col", axis=0, tiled=True)
+    receiver_block = refer_rounds(0, nodes)
     joined_weight = edge_w1.reshape(3 * width, width)
 
     def first_layer(rows, send_hot, recv_hot):

time: 347 us -> 332 us (0.957)
  waiting for transfers between devices: 124 us -> 97.1 us
  starting transfers between devices: 8.92 us -> 17.5 us
  matrix products: 83.5 us -> 88.4 us
    all_gather x1 -> x0, waiting for transfers between devices: 26.4 us -> none  [on_device(): receiver_block = lax.all_gather(nodes, 'col', axis=0, tiled=True)]
    all_to_all x0 -> x1, starting transfers between devices: none -> 8.65 us  [lax.all_to_all(jnp.stack(lax.axis_size('col') * [m], axis=0), 'col', 0, 0)]
    dot_general x10, matrix products: 22.4 us -> 27.3 us  [select_low(): jnp.dot(table_hot, table, preferred_element_type=jnp.float32)]
    while x40 -> x16, local copies, waits for them, and re-layouts: 7.65 us -> 7.65 us
  transfers between devices with their start and end apart: 3 -> 3, of which waited for: 3 -> 2; matrix products, arithmetic and copies ran while one was open for 2% -> 2% of each run, Pallas kernels for 0% -> 0%
where the time goes in v1:
time: 332 us; the launch traced here: 330 us
  waiting for transfers between devices  97.1 us (29%)
  matrix products  88.4 us (27%)
  local copies, waits for them, and re-layouts  68.4 us (21%)
  other arithmetic  29 us (9%)
  starting transfers between devices  17.5 us (5%)
  between operations  15 us (5%)
  blocking collectives  14.3 us (4%)
    psum x1, waiting for transfers between devices, on_device(): lax.psum(partial_value.astype(jnp.bfloat16), 'col').astype(jnp.float32)  85.8 us
    dot_general x10, matrix products, select_low(): jnp.dot(table_hot, table, preferred_element_type=jnp.float32)  27.3 us
    dot_general x4, matrix products, first_layer(): return jnp.dot(joined, joined_weight, preferred_element_type=jnp.float32)  20.7 us
    dot_general x6, matrix products, mlp_tail(): output = jnp.dot(hidden, second_weight, preferred_element_type=jnp.float32)  17.1 us
    dot_general x4, matrix products, edge_block(): lax.dot_general(recv_hot, kept, (((0,), (0,)), ((), ())), preferred_eleme...  16.6 us
    all_gather x1, blocking collectives, on_device(): sender_block = lax.all_gather(nodes, 'row', axis=0, tiled=True)  14.3 us
    all_to_all x1, waiting for transfers between devices, on_device(): lax.all_to_all(picked, ('row', 'col'), split_axis=0, concat_axis=0, tiled...  11.3 us
    reshape x1, local copies, waits for them, and re-layouts, on_device(): dec_pre.reshape(cells * fan_count, width)  10.8 us
  transfers between devices with their start and end apart: 3, of which 2 were waited for; matrix products, arithmetic and copies ran while one was open for 2% of the time, Pallas kernels for 0%

profile of v1, /device:TPU:1, one launch (start us, length us, event | category | flops | bytes accessed | tf_op | source)
XLA Modules:
  0.0 330.0 jit_solution(6802992136860983315)
XLA Ops:
  9.2 8.6 %all-to-all-start = ((bf16[16,64,512]{2,1,0:T(8,128)(2,1)}), bf16[16,64,512]{2,1,0:T(8,128)(2,1)}, u32[]{:S(2)}, u32[]{:S(2)}) async-start(bf16[16,64,512]{2,1,0:T(8,128)(2,1)} %stack.2), calls=%async_computation | async-start | bytes 2097152 | tf_op jit(solution)/shard_map/all_to_all | solution.py:9
  21.2 14.3 %all_gather.3 = bf16[512,512]{1,0:T(8,128)(2,1)S(1)} all-gather(bf16[64,512]{1,0:T(8,128)(2,1)S(1)} %copy-done.3), channel_id=1, replica_groups=mesh['row'=8,'col'=16] {'row'}, dimensions={0}, use_global_device_ids=true | all-gather | bytes 589824 | tf_op jit(solution)/shard_map/all_gather | solution.py:60
  35.5 104.0 %while.13 = (s32[]{:T(128)}, f32[1024,512]{1,0:T(8,128)}, bf16[4,1024,512]{2,1,0:T(8,128)(2,1)}, s32[4,1024]{1,0:T(4,128)S(1)}, pred[4,1024]{1,0:T(4,128)(4,1)S(...) while((s32[]{:T(128)}, f32[1024,512]{1,0:T(8,128)}, ...), condition=%wide.region_3.4_spmd.clone, body=%wide.region_0.3_spmd.clone.sunk | while | flops 4866973696 | bytes 44666096 | solution.py:97
  37.5 3.6 %fusion.95 = bf16[1024,512]{0,1:T(8,128)(2,1)} fusion(bf16[1024,512]{1,0:T(8,128)(2,1)} %get-tuple-element.306, s32[1024]{0:T(1024)S(1)} %bitcast.67), kind=kOutput, calls=%fused_computation.20.clone.1 | convolution fusion | flops 1075314688 | bytes 2101248 | tf_op jit(solution)/shard_map/while/body/eval_jaxpr/dot_general | solution.py:30
  44.0 5.2 %fusion.97 = f32[1024,512]{1,0:T(8,128)} fusion(bf16[1536,512]{1,0:T(8,128)(2,1)} %get-tuple-element.307, bf16[1024,512]{0,1:T(8,128)(2,1)} %fusion.95, bf16[1024,512]{0,1:T(8,128)(2,1)} %fusion.96, bf16[1024,512]{0,1:T(8,128)(2,1)S(1)} %bitcast.65), kind=kOutput, calls=%fused_computation.3.clone.1 | convolution fusion | flops 1620049920 | bytes 6815744 | tf_op jit(solution)/shard_map/while/body/eval_jaxpr/dot_general | solution.py:68
  49.1 2.9 fusion.98
  54.8 3.0 select_add_fusion.2
  62.3 3.6 %fusion.95 = bf16[1024,512]{0,1:T(8,128)(2,1)} fusion(bf16[1024,512]{1,0:T(8,128)(2,1)} %get-tuple-element.306, s32[1024]{0:T(1024)S(1)} %bitcast.67), kind=kOutput, calls=%fused_computation.20.clone.1 | convolution fusion | flops 1075314688 | bytes 2101248 | tf_op jit(solution)/shard_map/while/body/eval_jaxpr/dot_general | solution.py:30
  68.8 5.2 %fusion.97 = f32[1024,512]{1,0:T(8,128)} fusion(bf16[1536,512]{1,0:T(8,128)(2,1)} %get-tuple-element.307, bf16[1024,512]{0,1:T(8,128)(2,1)} %fusion.95, bf16[1024,512]{0,1:T(8,128)(2,1)} %fusion.96, bf16[1024,512]{0,1:T(8,128)(2,1)S(1)} %bitcast.65), kind=kOutput, calls=%fused_computation.3.clone.1 | convolution fusion | flops 1620049920 | bytes 6815744 | tf_op jit(solution)/shard_map/while/body/eval_jaxpr/dot_general | solution.py:68
  73.9 2.9 fusion.98
  79.6 4.6 %select_add_fusion.2 = f32[1024,512]{1,0:T(8,128)} fusion(f32[1024,512]{1,0:T(8,128)} %get-tuple-element.283, s32[1024]{0:T(1024)S(1)} %bitcast.68, pred[]{:T(512)S(6)} %compare.3, f32[1024,512]{0,1:T(8,128)S(1)} %get-tuple-element.264, f32[512]{0:T(512)S(1)} %get-tuple-element.311, f32[1024]{0:T(1024)S(1)} %add_rsqrt_fusion.4, ...), kind=kOutput, calls=%fused_computation.10.clone.1 | convolution fusion | flops 1079508992 | bytes 6306817 | tf_op jit(solution)/shard_map/while/body/eval_jaxpr/dot_general | solution.py:92
  88.7 3.6 %fusion.95 = bf16[1024,512]{0,1:T(8,128)(2,1)} fusion(bf16[1024,512]{1,0:T(8,128)(2,1)} %get-tuple-element.306, s32[1024]{0:T(1024)S(1)} %bitcast.67), kind=kOutput, calls=%fused_computation.20.clone.1 | convolution fusion | flops 1075314688 | bytes 2101248 | tf_op jit(solution)/shard_map/while/body/eval_jaxpr/dot_general | solution.py:30
  95.2 5.2 %fusion.97 = f32[1024,512]{1,0:T(8,128)} fusion(bf16[1536,512]{1,0:T(8,128)(2,1)} %get-tuple-element.307, bf16[1024,512]{0,1:T(8,128)(2,1)} %fusion.95, bf16[1024,512]{0,1:T(8,128)(2,1)} %fusion.96, bf16[1024,512]{0,1:T(8,128)(2,1)S(1)} %bitcast.65), kind=kOutput, calls=%fused_computation.3.clone.1 | convolution fusion | flops 1620049920 | bytes 6815744 | tf_op jit(solution)/shard_map/while/body/eval_jaxpr/dot_general | solution.py:68
  100.3 2.9 fusion.98
  106.0 4.5 %select_add_fusion.2 = f32[1024,512]{1,0:T(8,128)} fusion(f32[1024,512]{1,0:T(8,128)} %get-tuple-element.283, s32[1024]{0:T(1024)S(1)} %bitcast.68, pred[]{:T(512)S(6)} %compare.3, f32[1024,512]{0,1:T(8,128)S(1)} %get-tuple-element.264, f32[512]{0:T(512)S(1)} %get-tuple-element.311, f32[1024]{0:T(1024)S(1)} %add_rsqrt_fusion.4, ...), kind=kOutput, calls=%fused_computation.10.clone.1 | convolution fusion | flops 1079508992 | bytes 6306817 | tf_op jit(solution)/shard_map/while/body/eval_jaxpr/dot_general | solution.py:92
  115.1 3.6 %fusion.95 = bf16[1024,512]{0,1:T(8,128)(2,1)} fusion(bf16[1024,512]{1,0:T(8,128)(2,1)} %get-tuple-element.306, s32[1024]{0:T(1024)S(1)} %bitcast.67), kind=kOutput, calls=%fused_computation.20.clone.1 | convolution fusion | flops 1075314688 | bytes 2101248 | tf_op jit(solution)/shard_map/while/body/eval_jaxpr/dot_general | solution.py:30
  121.6 5.2 %fusion.97 = f32[1024,512]{1,0:T(8,128)} fusion(bf16[1536,512]{1,0:T(8,128)(2,1)} %get-tuple-element.307, bf16[1024,512]{0,1:T(8,128)(2,1)} %fusion.95, bf16[1024,512]{0,1:T(8,128)(2,1)} %fusion.96, bf16[1024,512]{0,1:T(8,128)(2,1)S(1)} %bitcast.65), kind=kOutput, calls=%fused_computation.3.clone.1 | convolution fusion | flops 1620049920 | bytes 6815744 | tf_op jit(solution)/shard_map/while/body/eval_jaxpr/dot_general | solution.py:68
  126.7 2.9 fusion.98
  132.4 4.5 %select_add_fusion.2 = f32[1024,512]{1,0:T(8,128)} fusion(f32[1024,512]{1,0:T(8,128)} %get-tuple-element.283, s32[1024]{0:T(1024)S(1)} %bitcast.68, pred[]{:T(512)S(6)} %compare.3, f32[1024,512]{0,1:T(8,128)S(1)} %get-tuple-element.264, f32[512]{0:T(512)S(1)} %get-tuple-element.311, f32[1024]{0:T(1024)S(1)} %add_rsqrt_fusion.4, ...), kind=kOutput, calls=%fused_computation.10.clone.1 | convolution fusion | flops 1079508992 | bytes 6306817 | tf_op jit(solution)/shard_map/while/body/eval_jaxpr/dot_general | solution.py:92
  139.5 2.8 convert_element_type.60
  142.8 85.8 %all-reduce.2.cloned.1.call-done = bf16[1024,512]{1,0:T(8,128)(2,1)} async-done(((bf16[1024,512]{1,0:T(8,128)(2,1)}), bf16[1024,512]{1,0:T(8,128)(2,1)}) %all-reduce.2.cloned.1.call-update) | async-done | bytes 1048592 | tf_op jit(solution)/shard_map/psum | solution.py:101
  231.6 8.8 %all-to-all-start.1 = ((bf16[128,4,512]{2,1,0:T(4,128)(2,1)}), bf16[128,4,512]{2,1,0:T(4,128)(2,1)S(1)}, u32[]{:S(2)}, u32[]{:S(2)}) async-start(bf16[128,4,512]{2,1,0:T(4,128)(2,1)} %reshape.86), calls=%async_computation.1 | async-start | bytes 1048576 | tf_op jit(solution)/shard_map/all_to_all | solution.py:115
  243.0 11.3 %all-to-all-done.1 = bf16[128,4,512]{2,1,0:T(4,128)(2,1)S(1)} async-done(((bf16[128,4,512]{2,1,0:T(4,128)(2,1)}), bf16[128,4,512]{2,1,0:T(4,128)(2,1)S(1)}, u32[]{:S(2)}, u32[]{:S(2)}) %all-to-all-start.1) | async-done | bytes 524320 | tf_op jit(solution)/shard_map/all_to_all | solution.py:115
  255.2 4.7 %fusion.28 = bf16[3072,512]{1,0:T(8,128)(2,1)} fusion(bf16[512,512]{1,0:T(8,128)(2,1)} %reshape.87, s32[3072]{0:T(1024)S(1)} %eq.75), kind=kOutput, calls=%fused_computation.43 | convolution fusion | flops 1613758464 | bytes 3682304 | tf_op jit(solution)/shard_map/dot_general | solution.py:30
  259.9 9.1 %dot_general.50 = bf16[1024,3,512]{2,1,0:T(4,128)(2,1)} reshape(bf16[3072,512]{1,0:T(8,128)(2,1)} %fusion.28) | data formatting | bytes 6291456 | tf_op jit(solution)/shard_map/dot_general | solution.py:122
  269.0 4.4 %broadcast_add_fusion = f32[1024,3,512]{2,0,1:T(8,128)S(1)} fusion(f32[1024,512]{1,0:T(8,128)S(1)} %fusion.36, bf16[1024,3,512]{2,1,0:T(4,128)(2,1)} %dot_general.50, bf16[2,512,512]{2,1,0:T(8,128)(2,1)} %param.37), kind=kOutput, calls=%fused_computation.47 | convolution fusion | flops 1612185600 | bytes 13107200 | tf_op jit(solution)/shard_map/dot_general | solution.py:122
  273.4 7.5 %copy.29 = f32[1024,3,512]{2,1,0:T(4,128)} copy(f32[1024,3,512]{2,0,1:T(8,128)S(1)} %broadcast_add_fusion) | data formatting | bytes 12582912 | tf_op jit(solution)/shard_map/add | solution.py:126
  281.0 10.8 %reshape.88 = f32[3072,512]{1,0:T(8,128)} reshape(f32[1024,3,512]{2,1,0:T(4,128)} %copy.29) | data formatting | bytes 12582912 | tf_op jit(solution)/shard_map/reshape | solution.py:127
  291.7 4.2 %fusion.62 = (f32[3072]{0:T(1024)S(1)}, f32[3072,512]{1,0:T(8,128)S(1)}) fusion(bf16[512,512]{1,0:T(8,128)(2,1)S(1)} %copy-done, f32[3072,512]{1,0:T(8,128)} %reshape.88), kind=kOutput, calls=%fused_computation.81 | convolution fusion | flops 1620046848 | bytes 13119488 | tf_op jit(solution)/shard_map/dot_general | solution.py:21
  297.9 3.8 %multiply_multiply_fusion = f32[3072,512]{1,0:T(8,128)} fusion(f32[3072,512]{1,0:T(8,128)S(1)} %get-tuple-element.172, f32[512]{0:T(512)S(1)} %copy-done.12, f32[3072]{0:T(1024)S(1)} %add_rsqrt_fusion.1, f32[3072]{0:T(1024)S(1)} %broadcast_multiply_fusion.1), kind=kLoop, calls=%fused_computation.38 | loop fusion | flops 4718592 | bytes 12609536 | tf_op jit(solution)/shard_map/mul | solution.py:16
  301.7 10.5 %reshape.89 = f32[1024,3,512]{2,1,0:T(4,128)} reshape(f32[3072,512]{1,0:T(8,128)} %multiply_multiply_fusion) | data formatting | bytes 12582912 | tf_op jit(solution)/shard_map/reshape | solution.py:127
  312.2 8.4 %reduce_sum.67 = f32[1024,512]{1,0:T(8,128)S(1)} reduce(f32[1024,3,512]{2,1,0:T(4,128)} %reshape.89, f32[]{:T(128)} %constant.51.clone.1), dimensions={1}, to_apply=%region_9.10 | reduce | flops 1048576 | bytes 8388612 | tf_op jit(solution)/shard_map/reduce_sum | solution.py:130
  (124 shorter events, 56.2 us)
Async XLA Ops:
  7.2 284.6 %copy-start = (bf16[512,512]{1,0:T(8,128)(2,1)S(1)}, bf16[512,512]{1,0:T(8,128)(2,1)}, u32[]{:S(2)}) copy-start(bf16[512,512]{1,0:T(8,128)(2,1)} %param.38) | copy-start | bytes 1572868
  7.2 14.0 %copy-start.3 = (bf16[64,512]{1,0:T(8,128)(2,1)S(1)}, bf16[64,512]{1,0:T(8,128)(2,1)}, u32[]{:S(2)}) copy-start(bf16[64,512]{1,0:T(8,128)(2,1)} %param.21) | copy-start | bytes 196612
  7.2 12.0 %copy-start.8 = (s32[1,1,4096]{2,1,0:T(1,128)S(1)}, s32[1,1,4096]{2,1,0:T(1,128)}, u32[]{:S(2)}) copy-start(s32[1,1,4096]{2,1,0:T(1,128)} %param.23) | copy-start | bytes 49156
  7.2 12.6 %copy-start.9 = (s32[1,1,4096]{2,1,0:T(1,128)S(1)}, s32[1,1,4096]{2,1,0:T(1,128)}, u32[]{:S(2)}) copy-start(s32[1,1,4096]{2,1,0:T(1,128)} %param.24) | copy-start | bytes 49156
  7.2 13.3 %copy-start.10 = (s32[1,1,4096]{2,1,0:T(1,128)S(1)}, s32[1,1,4096]{2,1,0:T(1,128)}, u32[]{:S(2)}) copy-start(s32[1,1,4096]{2,1,0:T(1,128)} %param.25) | copy-start | bytes 49156
  7.2 28.2 %copy-start.6 = (f32[512]{0:T(512)S(1)}, f32[512]{0:T(512)}, u32[]{:S(2)}) copy-start(f32[512]{0:T(512)} %param.30) | copy-start | bytes 6148
  7.2 28.2 %copy-start.15 = (bf16[7,512]{1,0:T(8,128)(2,1)S(1)}, bf16[7,512]{1,0:T(8,128)(2,1)}, u32[]{:S(2)}) copy-start(bf16[7,512]{1,0:T(8,128)(2,1)} %param.28) | copy-start | bytes 21508
  9.2 26.2 %all-to-all-start = ((bf16[16,64,512]{2,1,0:T(8,128)(2,1)}), bf16[16,64,512]{2,1,0:T(8,128)(2,1)}, u32[]{:S(2)}, u32[]{:S(2)}) async-start(bf16[16,64,512]{2,1,0:T(8,128)(2,1)} %stack.2), calls=%async_computation | async-start | bytes 2097152 | tf_op jit(solution)/shard_map/all_to_all | solution.py:9
  17.9 210.7 %all-reduce.2.cloned.1.call-start = ((), (), s32[]{:S(2)}) async-start(), calls=%async_computation.2 | async-start | bytes 2097152 | tf_op jit(solution)/shard_map/psum | solution.py:101
  43.0 1.0 copy-start.1
  52.0 1.2 copy-start.2
  67.8 1.0 copy-start.1
  76.8 1.2 copy-start.2
  94.2 1.0 copy-start.1
  103.3 1.2 copy-start.2
  120.6 1.0 copy-start.1
  129.7 1.2 copy-start.2
  139.5 2.9 copy-start.13
  139.5 3.1 copy-start.4
  139.5 89.1 %copy-start.14 = (bf16[512,512]{1,0:T(8,128)(2,1)S(1)}, bf16[512,512]{1,0:T(8,128)(2,1)}, u32[]{:S(2)}) copy-start(bf16[512,512]{1,0:T(8,128)(2,1)} %param.32) | copy-start | bytes 1572868
  142.3 87.9 %copy-start.11 = (f32[512]{0:T(512)S(1)}, f32[512]{0:T(512)}, u32[]{:S(2)}) copy-start(f32[512]{0:T(512)} %param.33) | copy-start | bytes 6148
  142.8 97.6 %copy-start.7 = (s32[1024,3]{0,1:T(4,128)S(1)}, s32[1024,3]{0,1:T(4,128)}, u32[]{:S(2)}) copy-start(s32[1024,3]{0,1:T(4,128)} %param.36) | copy-start | bytes 36868
  230.3 12.7 %copy-start.5 = (bf16[64,512]{1,0:T(8,128)(2,1)}, bf16[64,512]{1,0:T(8,128)(2,1)S(1)}, u32[]{:S(2)}) copy-start(bf16[64,512]{1,0:T(8,128)(2,1)S(1)} %add_convert_fusion.2) | copy-start | bytes 196612
  231.6 22.7 %all-to-all-start.1 = ((bf16[128,4,512]{2,1,0:T(4,128)(2,1)}), bf16[128,4,512]{2,1,0:T(4,128)(2,1)S(1)}, u32[]{:S(2)}, u32[]{:S(2)}) async-start(bf16[128,4,512]{2,1,0:T(4,128)(2,1)} %reshape.86), calls=%async_computation.1 | async-start | bytes 1048576 | tf_op jit(solution)/shard_map/all_to_all | solution.py:115
  295.9 2.0 copy-start.12
Sparse Core Ops, SparseCore 0:
  142.4 86.1 all-reduce.1
